TPU v7x, 128 devices: a whole 4x4x4 slice. The times are simulated.
128 devices in a mesh: blk: 32 (over y, x_hi, z), head: 4 (over x_lo, core).
Axes of the slice: x: 4 (x_hi: 2, x_lo: 2; x = x_hi * 2 + x_lo), y: 4, z: 4, core: 2. Of those that a mesh axis runs over, the one named last changes fastest.
Arguments:
- img_qkv: bfloat16 [12288, 9216], P(('blk', 'head')), may hold values from -6 to 6
- txt_qkv: bfloat16 [512, 9216], P(('blk', 'head')), may hold values from -6 to 6
- q_gain: float32 [128], replicated, may hold values from 1.4 to 6.5
- k_gain: float32 [128], replicated, may hold values from 1.4 to 6.5
Outputs:
- img_out: bfloat16 [12288, 3072], P(('blk', 'head'))
- txt_out: bfloat16 [512, 3072], P(('blk', 'head'))
All inputs are finite; a program needn't handle non-finite values.
Results may differ from a plain program's by a relative error of at most 0.0065.
The roundings to bfloat16 on the way count: a program that leaves them out, or rounds other values in their place, can miss the bound.
Values may be sent and summed in bfloat16 or wider, within the bound.
A program may use at most 128 MiB of HBM per device.

v0:
```python
import jax
import jax.numpy as jnp
from jax import lax
from jax.sharding import PartitionSpec as P

HEADS = 24
GRID_W = 128


EPSILON = 1e-06


def normalize(projected, gains):
    projected = projected.astype(jnp.float32)
    return (
        projected
        * lax.rsqrt(jnp.mean(projected * projected, axis=-1, keepdims=True) + EPSILON)
        * gains
    )


def axis_freqs(pair_count):
    return 10000.0 ** (-(jnp.arange(pair_count, dtype=jnp.float32) / pair_count))


def rope_angles(token_index, half_img, head_dim):
    frame_pairs = head_dim // 16
    side_pairs = (head_dim // 2 - frame_pairs) // 2
    frame_pos = (token_index // half_img).astype(jnp.float32)
    within = token_index % half_img
    row_pos = (within // GRID_W).astype(jnp.float32)
    col_pos = (within % GRID_W).astype(jnp.float32)
    return jnp.concatenate(
        [
            frame_pos[:, None] * axis_freqs(frame_pairs)[None, :],
            row_pos[:, None] * axis_freqs(side_pairs)[None, :],
            col_pos[:, None] * axis_freqs(side_pairs)[None, :],
        ],
        axis=1,
    )


def rotate(projected, angles):
    tokens_here, heads_here, dims_here = projected.shape
    pairs = projected.reshape(tokens_here, heads_here, dims_here // 2, 2)
    cosine = jnp.cos(angles)[:, None, :]
    sine = jnp.sin(angles)[:, None, :]
    first = pairs[..., 0]
    second = pairs[..., 1]
    return jnp.stack(
        [cosine * first - sine * second, sine * first + cosine * second], axis=-1
    ).reshape(projected.shape)


def prepare(parts, query_gain, key_gain, angles):
    query_rows = normalize(parts[:, 0], query_gain)
    key_rows = normalize(parts[:, 1], key_gain)
    if angles is not None:
        query_rows = rotate(query_rows, angles)
        key_rows = rotate(key_rows, angles)
    return jnp.stack(
        [query_rows.astype(jnp.bfloat16), key_rows.astype(jnp.bfloat16), parts[:, 2]], axis=1
    )


def absorb(queries, running, key_block, value_block):
    running_top, running_sum, running_out = running
    score_scale = queries.shape[2] ** (-0.5)
    scores = (
        jnp.einsum("qhd,khd->qhk", queries, key_block, preferred_element_type=jnp.float32)
        * score_scale
    )
    new_top = jnp.maximum(running_top, jnp.max(scores, axis=-1))
    rescale = jnp.exp(running_top - new_top)
    weights = jnp.exp(scores - new_top[..., None])
    new_sum = running_sum * rescale + jnp.sum(weights, axis=-1)
    product = jnp.einsum(
        "qhk,khd->qhd",
        weights.astype(jnp.bfloat16),
        value_block,
        preferred_element_type=jnp.float32,
    )
    return (new_top, new_sum, running_out * rescale[..., None] + product)


def start_state(queries):
    query_count, heads_here, head_dim = queries.shape
    return (
        jnp.full((query_count, heads_here), -jnp.inf, jnp.float32),
        jnp.zeros((query_count, heads_here), jnp.float32),
        jnp.zeros((query_count, heads_here, head_dim), jnp.float32),
    )


def finish(state):
    top_score, weight_sum, weighted = state
    return (weighted / weight_sum[..., None]).astype(jnp.bfloat16)


def local(img_qkv, txt_qkv, q_gain, k_gain):
    groups = lax.axis_size("head")
    img_rows = img_qkv.shape[0]
    txt_rows = txt_qkv.shape[0]
    model_width = img_qkv.shape[1] // 3
    head_dim = model_width // HEADS
    local_heads = HEADS // groups
    local_width = local_heads * head_dim
    group_img = groups * img_rows
    group_txt = groups * txt_rows
    half_img = img_rows * groups * lax.axis_size("blk") // 2
    group_base = lax.axis_index("blk") * group_img
    img_moved, txt_moved = (
        lax.all_to_all(
            img_qkv.reshape(img_rows, 3, groups, local_width),
            "head",
            split_axis=2,
            concat_axis=0,
            tiled=True,
        ),
        lax.all_to_all(
            txt_qkv.reshape(txt_rows, 3, groups, local_width),
            "head",
            split_axis=2,
            concat_axis=0,
            tiled=True,
        ),
    )
    group_index = group_base + jnp.arange(group_img, dtype=jnp.int32)
    image_parts = prepare(
        img_moved.reshape(group_img, 3, local_heads, head_dim),
        q_gain,
        k_gain,
        rope_angles(group_index, half_img, head_dim),
    )
    text_parts = prepare(
        txt_moved.reshape(group_txt, 3, local_heads, head_dim), q_gain, k_gain, None
    )
    queries = jnp.concatenate([text_parts[:, 0], image_parts[:, 0]], axis=0)
    keys_here = jnp.concatenate([text_parts[:, 1], image_parts[:, 1]], axis=0)
    values_here = jnp.concatenate([text_parts[:, 2], image_parts[:, 2]], axis=0)
    shard_rows = keys_here.shape[0]
    all_keys, all_values = (
        lax.all_gather(keys_here, "blk", axis=0, tiled=True),
        lax.all_gather(values_here, "blk", axis=0, tiled=True),
    )
    piece_rows = all_keys.shape[0]
    shard_count = piece_rows // shard_rows
    per_step = 4
    step_rows = per_step * shard_rows
    turns = shard_count // per_step

    def absorb_step(state_now, block_pair):
        return (absorb(queries, state_now, block_pair[0], block_pair[1]), None)

    scanned, unused = lax.scan(
        absorb_step,
        start_state(queries),
        (
            all_keys.reshape(turns, step_rows, local_heads, head_dim),
            all_values.reshape(turns, step_rows, local_heads, head_dim),
        ),
    )
    attended = finish(scanned).reshape(group_txt + group_img, local_width)
    img_attended = attended[group_txt:]
    txt_attended = attended[:group_txt]
    img_home, txt_home = (
        lax.all_to_all(
            img_attended.reshape(group_img, 1, local_width),
            "head",
            split_axis=0,
            concat_axis=1,
            tiled=True,
        ),
        lax.all_to_all(
            txt_attended.reshape(group_txt, 1, local_width),
            "head",
            split_axis=0,
            concat_axis=1,
            tiled=True,
        ),
    )
    return (img_home.reshape(img_rows, model_width), txt_home.reshape(txt_rows, model_width))


def solution(mesh):
    in_specs = (P(("blk", "head"), None), P(("blk", "head"), None), P(), P())
    out_specs = (P(("blk", "head"), None), P(("blk", "head"), None))
    return jax.shard_map(local, mesh=mesh, in_specs=in_specs, out_specs=out_specs, check_vma=False)
```

profile of v0, /device:TPU:1, one launch (start us, length us, event | category | flops | bytes accessed | tf_op | source)
XLA Modules:
  0.0 664.8 jit_solution(8033369753489552014)
XLA Ops:
  7.2 0.9 reshape.243
  8.1 0.7 copy.73
  8.7 4.7 all-to-all-start
  13.5 3.0 reshape.245
  16.5 1.5 copy.75
  18.0 0.8 mul.232
  18.7 0.7 mul.248
  19.5 3.6 all-to-all-start.1
  23.3 1.1 fusion.33
  24.6 0.7 fusion.31
  25.3 0.8 copy.79
  26.1 18.3 %all-to-all-done.1 = bf16[96,3,4,768]{3,0,1,2:T(8,128)(2,1)S(1)} async-done(((bf16[96,3,4,768]{3,0,1,2:T(8,128)(2,1)}), bf16[96,3,4,768]{3,0,1,2:T(8,128)(2,1)S(1)}, u32[]{:S(2)}, u32[]{:S(2)}) %all-to-all-start.1) | async-done | bytes 1769504 | tf_op jit(solution)/shard_map/all_to_all | solution.py:113
  44.4 1.3 copy.76
  45.8 3.6 reshape.246
  49.4 2.0 slice_bitcast_fusion
  51.4 1.6 multiply_reduce_fusion
  52.9 2.8 copy.77
  55.8 2.1 reshape.254
  57.9 1.5 copy.81
  59.4 2.0 reshape.256
  61.7 1.9 multiply_multiply_fusion
  63.6 3.1 subtract_convert_fusion
  66.7 1.3 pad_maximum_fusion.3
  68.7 1.1 copy.80
  70.0 0.8 slice_bitcast_fusion.1
  71.0 1.0 copy.84
  72.2 1.3 pad_maximum_fusion.4
  74.5 171.4 %all-gather.3.cloned.1.call-done = bf16[12800,6,128]{2,0,1:T(8,128)(2,1)} async-done(((bf16[400,6,128]{2,0,1:T(8,128)(2,1)}), bf16[12800,6,128]{2,0,1:T(8,128)(2,1)}) %all-gather.3.cloned.1.call-update) | async-done | bytes 19660816 | tf_op jit(solution)/shard_map/all_gather | solution.py:143
  245.9 174.7 %all-gather.5.cloned.1.call-done = bf16[12800,6,128]{2,0,1:T(8,128)(2,1)} async-done(((bf16[400,6,128]{2,0,1:T(8,128)(2,1)}), bf16[12800,6,128]{2,0,1:T(8,128)(2,1)}) %all-gather.5.cloned.1.call-update) | async-done | bytes 19660816 | tf_op jit(solution)/shard_map/all_gather | solution.py:144
  420.6 212.2 %while.15 = (s32[]{:T(128)}, f32[400,6]{0,1:T(8,128)S(1)}, f32[400,6]{0,1:T(8,128)S(1)}, f32[400,6,128]{2,0,1:T(8,128)S(1)}, bf16[8,1600,6,128]{3,1,0,2:T(8,128)...) while((s32[]{:T(128)}, f32[400,6]{0,1:T(8,128)S(1)}, ...), condition=%wide.region_7.8_spmd.clone, body=%wide.region_4.7_spmd.clone.sunk | while | flops 1997733632 | bytes 54836324 | solution.py:155
  420.6 9.7 %bitcast_reduce_fusion.2 = (f32[400,6]{0,1:T(8,128)S(1)}, f32[6,1600,400]{1,2,0:T(8,128)}) fusion(bf16[400,6,128]{2,0,1:T(8,128)(2,1)S(1)} %get-tuple-element.218, bf16[8,1600,6,128]{3,1,0,2:T(8,128)(2,1)} %get-tuple-element.217, s32[]{:T(128)} %get-tuple-element.204), kind=kOutput, calls=%fused_computation.1.clone.1 | convolution fusion | flops 990717568 | bytes 18442112 | tf_op jit(solution)/shard_map/while/body/eval_jaxpr/qhd,khd->qhk/dot_general | solution.py:70
  430.3 8.3 %fusion.53 = f32[400,6]{0,1:T(8,128)S(1)} fusion(f32[6,1600,400]{1,2,0:T(8,128)} %get-tuple-element.192, f32[400,6]{0,1:T(8,128)S(1)} %select_maximum_fusion.2), kind=kLoop, calls=%fused_computation.4.clone.1 | loop fusion | flops 11517600 | bytes 15379200 | tf_op jit(solution)/shard_map/while/body/eval_jaxpr/reduce_sum | solution.py:76
  438.6 8.4 %fusion.55 = f32[400,6,128]{2,0,1:T(8,128)S(1)} fusion(bf16[8,1600,6,128]{3,1,0,2:T(8,128)(2,1)} %get-tuple-element.219, s32[]{:T(128)} %get-tuple-element.204, f32[6,1600,400]{1,2,0:T(8,128)} %get-tuple-element.192, f32[400,6]{0,1:T(8,128)S(1)} %select_maximum_fusion.2, f32[400,6,128]{2,0,1:T(8,128)S(1)} %get-tuple-element.207, ...), kind=kOutput, calls=%fused_computation.14.clone.1 | convolution fusion | flops 995481600 | bytes 20909312 | tf_op jit(solution)/shard_map/while/body/eval_jaxpr/qhk,khd->qhd/dot_general | solution.py:77
  447.1 9.7 %bitcast_reduce_fusion.2 = (f32[400,6]{0,1:T(8,128)S(1)}, f32[6,1600,400]{1,2,0:T(8,128)}) fusion(bf16[400,6,128]{2,0,1:T(8,128)(2,1)S(1)} %get-tuple-element.218, bf16[8,1600,6,128]{3,1,0,2:T(8,128)(2,1)} %get-tuple-element.217, s32[]{:T(128)} %get-tuple-element.204), kind=kOutput, calls=%fused_computation.1.clone.1 | convolution fusion | flops 990717568 | bytes 18442112 | tf_op jit(solution)/shard_map/while/body/eval_jaxpr/qhd,khd->qhk/dot_general | solution.py:70
  456.8 8.3 %fusion.53 = f32[400,6]{0,1:T(8,128)S(1)} fusion(f32[6,1600,400]{1,2,0:T(8,128)} %get-tuple-element.192, f32[400,6]{0,1:T(8,128)S(1)} %select_maximum_fusion.2), kind=kLoop, calls=%fused_computation.4.clone.1 | loop fusion | flops 11517600 | bytes 15379200 | tf_op jit(solution)/shard_map/while/body/eval_jaxpr/reduce_sum | solution.py:76
  465.2 8.4 %fusion.55 = f32[400,6,128]{2,0,1:T(8,128)S(1)} fusion(bf16[8,1600,6,128]{3,1,0,2:T(8,128)(2,1)} %get-tuple-element.219, s32[]{:T(128)} %get-tuple-element.204, f32[6,1600,400]{1,2,0:T(8,128)} %get-tuple-element.192, f32[400,6]{0,1:T(8,128)S(1)} %select_maximum_fusion.2, f32[400,6,128]{2,0,1:T(8,128)S(1)} %get-tuple-element.207, ...), kind=kOutput, calls=%fused_computation.14.clone.1 | convolution fusion | flops 995481600 | bytes 20909312 | tf_op jit(solution)/shard_map/while/body/eval_jaxpr/qhk,khd->qhd/dot_general | solution.py:77
  473.6 9.7 %bitcast_reduce_fusion.2 = (f32[400,6]{0,1:T(8,128)S(1)}, f32[6,1600,400]{1,2,0:T(8,128)}) fusion(bf16[400,6,128]{2,0,1:T(8,128)(2,1)S(1)} %get-tuple-element.218, bf16[8,1600,6,128]{3,1,0,2:T(8,128)(2,1)} %get-tuple-element.217, s32[]{:T(128)} %get-tuple-element.204), kind=kOutput, calls=%fused_computation.1.clone.1 | convolution fusion | flops 990717568 | bytes 18442112 | tf_op jit(solution)/shard_map/while/body/eval_jaxpr/qhd,khd->qhk/dot_general | solution.py:70
  483.3 8.3 %fusion.53 = f32[400,6]{0,1:T(8,128)S(1)} fusion(f32[6,1600,400]{1,2,0:T(8,128)} %get-tuple-element.192, f32[400,6]{0,1:T(8,128)S(1)} %select_maximum_fusion.2), kind=kLoop, calls=%fused_computation.4.clone.1 | loop fusion | flops 11517600 | bytes 15379200 | tf_op jit(solution)/shard_map/while/body/eval_jaxpr/reduce_sum | solution.py:76
  491.7 8.4 %fusion.55 = f32[400,6,128]{2,0,1:T(8,128)S(1)} fusion(bf16[8,1600,6,128]{3,1,0,2:T(8,128)(2,1)} %get-tuple-element.219, s32[]{:T(128)} %get-tuple-element.204, f32[6,1600,400]{1,2,0:T(8,128)} %get-tuple-element.192, f32[400,6]{0,1:T(8,128)S(1)} %select_maximum_fusion.2, f32[400,6,128]{2,0,1:T(8,128)S(1)} %get-tuple-element.207, ...), kind=kOutput, calls=%fused_computation.14.clone.1 | convolution fusion | flops 995481600 | bytes 20909312 | tf_op jit(solution)/shard_map/while/body/eval_jaxpr/qhk,khd->qhd/dot_general | solution.py:77
  500.2 9.7 %bitcast_reduce_fusion.2 = (f32[400,6]{0,1:T(8,128)S(1)}, f32[6,1600,400]{1,2,0:T(8,128)}) fusion(bf16[400,6,128]{2,0,1:T(8,128)(2,1)S(1)} %get-tuple-element.218, bf16[8,1600,6,128]{3,1,0,2:T(8,128)(2,1)} %get-tuple-element.217, s32[]{:T(128)} %get-tuple-element.204), kind=kOutput, calls=%fused_computation.1.clone.1 | convolution fusion | flops 990717568 | bytes 18442112 | tf_op jit(solution)/shard_map/while/body/eval_jaxpr/qhd,khd->qhk/dot_general | solution.py:70
  509.8 8.3 %fusion.53 = f32[400,6]{0,1:T(8,128)S(1)} fusion(f32[6,1600,400]{1,2,0:T(8,128)} %get-tuple-element.192, f32[400,6]{0,1:T(8,128)S(1)} %select_maximum_fusion.2), kind=kLoop, calls=%fused_computation.4.clone.1 | loop fusion | flops 11517600 | bytes 15379200 | tf_op jit(solution)/shard_map/while/body/eval_jaxpr/reduce_sum | solution.py:76
  518.2 8.4 %fusion.55 = f32[400,6,128]{2,0,1:T(8,128)S(1)} fusion(bf16[8,1600,6,128]{3,1,0,2:T(8,128)(2,1)} %get-tuple-element.219, s32[]{:T(128)} %get-tuple-element.204, f32[6,1600,400]{1,2,0:T(8,128)} %get-tuple-element.192, f32[400,6]{0,1:T(8,128)S(1)} %select_maximum_fusion.2, f32[400,6,128]{2,0,1:T(8,128)S(1)} %get-tuple-element.207, ...), kind=kOutput, calls=%fused_computation.14.clone.1 | convolution fusion | flops 995481600 | bytes 20909312 | tf_op jit(solution)/shard_map/while/body/eval_jaxpr/qhk,khd->qhd/dot_general | solution.py:77
  526.7 9.7 %bitcast_reduce_fusion.2 = (f32[400,6]{0,1:T(8,128)S(1)}, f32[6,1600,400]{1,2,0:T(8,128)}) fusion(bf16[400,6,128]{2,0,1:T(8,128)(2,1)S(1)} %get-tuple-element.218, bf16[8,1600,6,128]{3,1,0,2:T(8,128)(2,1)} %get-tuple-element.217, s32[]{:T(128)} %get-tuple-element.204), kind=kOutput, calls=%fused_computation.1.clone.1 | convolution fusion | flops 990717568 | bytes 18442112 | tf_op jit(solution)/shard_map/while/body/eval_jaxpr/qhd,khd->qhk/dot_general | solution.py:70
  536.4 8.3 %fusion.53 = f32[400,6]{0,1:T(8,128)S(1)} fusion(f32[6,1600,400]{1,2,0:T(8,128)} %get-tuple-element.192, f32[400,6]{0,1:T(8,128)S(1)} %select_maximum_fusion.2), kind=kLoop, calls=%fused_computation.4.clone.1 | loop fusion | flops 11517600 | bytes 15379200 | tf_op jit(solution)/shard_map/while/body/eval_jaxpr/reduce_sum | solution.py:76
  544.7 8.4 %fusion.55 = f32[400,6,128]{2,0,1:T(8,128)S(1)} fusion(bf16[8,1600,6,128]{3,1,0,2:T(8,128)(2,1)} %get-tuple-element.219, s32[]{:T(128)} %get-tuple-element.204, f32[6,1600,400]{1,2,0:T(8,128)} %get-tuple-element.192, f32[400,6]{0,1:T(8,128)S(1)} %select_maximum_fusion.2, f32[400,6,128]{2,0,1:T(8,128)S(1)} %get-tuple-element.207, ...), kind=kOutput, calls=%fused_computation.14.clone.1 | convolution fusion | flops 995481600 | bytes 20909312 | tf_op jit(solution)/shard_map/while/body/eval_jaxpr/qhk,khd->qhd/dot_general | solution.py:77
  553.2 9.7 %bitcast_reduce_fusion.2 = (f32[400,6]{0,1:T(8,128)S(1)}, f32[6,1600,400]{1,2,0:T(8,128)}) fusion(bf16[400,6,128]{2,0,1:T(8,128)(2,1)S(1)} %get-tuple-element.218, bf16[8,1600,6,128]{3,1,0,2:T(8,128)(2,1)} %get-tuple-element.217, s32[]{:T(128)} %get-tuple-element.204), kind=kOutput, calls=%fused_computation.1.clone.1 | convolution fusion | flops 990717568 | bytes 18442112 | tf_op jit(solution)/shard_map/while/body/eval_jaxpr/qhd,khd->qhk/dot_general | solution.py:70
  562.9 8.3 %fusion.53 = f32[400,6]{0,1:T(8,128)S(1)} fusion(f32[6,1600,400]{1,2,0:T(8,128)} %get-tuple-element.192, f32[400,6]{0,1:T(8,128)S(1)} %select_maximum_fusion.2), kind=kLoop, calls=%fused_computation.4.clone.1 | loop fusion | flops 11517600 | bytes 15379200 | tf_op jit(solution)/shard_map/while/body/eval_jaxpr/reduce_sum | solution.py:76
  571.3 8.4 %fusion.55 = f32[400,6,128]{2,0,1:T(8,128)S(1)} fusion(bf16[8,1600,6,128]{3,1,0,2:T(8,128)(2,1)} %get-tuple-element.219, s32[]{:T(128)} %get-tuple-element.204, f32[6,1600,400]{1,2,0:T(8,128)} %get-tuple-element.192, f32[400,6]{0,1:T(8,128)S(1)} %select_maximum_fusion.2, f32[400,6,128]{2,0,1:T(8,128)S(1)} %get-tuple-element.207, ...), kind=kOutput, calls=%fused_computation.14.clone.1 | convolution fusion | flops 995481600 | bytes 20909312 | tf_op jit(solution)/shard_map/while/body/eval_jaxpr/qhk,khd->qhd/dot_general | solution.py:77
  579.7 9.7 %bitcast_reduce_fusion.2 = (f32[400,6]{0,1:T(8,128)S(1)}, f32[6,1600,400]{1,2,0:T(8,128)}) fusion(bf16[400,6,128]{2,0,1:T(8,128)(2,1)S(1)} %get-tuple-element.218, bf16[8,1600,6,128]{3,1,0,2:T(8,128)(2,1)} %get-tuple-element.217, s32[]{:T(128)} %get-tuple-element.204), kind=kOutput, calls=%fused_computation.1.clone.1 | convolution fusion | flops 990717568 | bytes 18442112 | tf_op jit(solution)/shard_map/while/body/eval_jaxpr/qhd,khd->qhk/dot_general | solution.py:70
  589.4 8.3 %fusion.53 = f32[400,6]{0,1:T(8,128)S(1)} fusion(f32[6,1600,400]{1,2,0:T(8,128)} %get-tuple-element.192, f32[400,6]{0,1:T(8,128)S(1)} %select_maximum_fusion.2), kind=kLoop, calls=%fused_computation.4.clone.1 | loop fusion | flops 11517600 | bytes 15379200 | tf_op jit(solution)/shard_map/while/body/eval_jaxpr/reduce_sum | solution.py:76
  597.8 8.4 %fusion.55 = f32[400,6,128]{2,0,1:T(8,128)S(1)} fusion(bf16[8,1600,6,128]{3,1,0,2:T(8,128)(2,1)} %get-tuple-element.219, s32[]{:T(128)} %get-tuple-element.204, f32[6,1600,400]{1,2,0:T(8,128)} %get-tuple-element.192, f32[400,6]{0,1:T(8,128)S(1)} %select_maximum_fusion.2, f32[400,6,128]{2,0,1:T(8,128)S(1)} %get-tuple-element.207, ...), kind=kOutput, calls=%fused_computation.14.clone.1 | convolution fusion | flops 995481600 | bytes 20909312 | tf_op jit(solution)/shard_map/while/body/eval_jaxpr/qhk,khd->qhd/dot_general | solution.py:77
  606.3 9.7 %bitcast_reduce_fusion.2 = (f32[400,6]{0,1:T(8,128)S(1)}, f32[6,1600,400]{1,2,0:T(8,128)}) fusion(bf16[400,6,128]{2,0,1:T(8,128)(2,1)S(1)} %get-tuple-element.218, bf16[8,1600,6,128]{3,1,0,2:T(8,128)(2,1)} %get-tuple-element.217, s32[]{:T(128)} %get-tuple-element.204), kind=kOutput, calls=%fused_computation.1.clone.1 | convolution fusion | flops 990717568 | bytes 18442112 | tf_op jit(solution)/shard_map/while/body/eval_jaxpr/qhd,khd->qhk/dot_general | solution.py:70
  616.0 8.3 %fusion.53 = f32[400,6]{0,1:T(8,128)S(1)} fusion(f32[6,1600,400]{1,2,0:T(8,128)} %get-tuple-element.192, f32[400,6]{0,1:T(8,128)S(1)} %select_maximum_fusion.2), kind=kLoop, calls=%fused_computation.4.clone.1 | loop fusion | flops 11517600 | bytes 15379200 | tf_op jit(solution)/shard_map/while/body/eval_jaxpr/reduce_sum | solution.py:76
  624.3 8.4 %fusion.55 = f32[400,6,128]{2,0,1:T(8,128)S(1)} fusion(bf16[8,1600,6,128]{3,1,0,2:T(8,128)(2,1)} %get-tuple-element.219, s32[]{:T(128)} %get-tuple-element.204, f32[6,1600,400]{1,2,0:T(8,128)} %get-tuple-element.192, f32[400,6]{0,1:T(8,128)S(1)} %select_maximum_fusion.2, f32[400,6,128]{2,0,1:T(8,128)S(1)} %get-tuple-element.207, ...), kind=kOutput, calls=%fused_computation.14.clone.1 | convolution fusion | flops 995481600 | bytes 20909312 | tf_op jit(solution)/shard_map/while/body/eval_jaxpr/qhk,khd->qhd/dot_general | solution.py:77
  634.0 0.7 reduce.4
  634.9 0.6 reshape.260
  635.5 4.3 all-to-all-start.3
  640.1 1.0 reduce.3
  641.4 1.0 reshape.258
  642.4 0.6 all-to-all-done.3
  643.0 4.2 all-to-all-start.2
  647.4 0.6 all_to_all.54
  648.0 7.9 %all-to-all-done.2 = bf16[4,2,36864]{2,1,0:T(2,128)(2,1)S(1)} async-done(((bf16[4,2,36864]{2,1,0:T(2,128)(2,1)}), bf16[4,2,36864]{2,1,0:T(2,128)(2,1)S(1)}, u32[]{:S(2)}, u32[]{:S(2)}) %all-to-all-start.2) | async-done | bytes 589856 | tf_op jit(solution)/shard_map/all_to_all | solution.py:167
  657.0 0.9 copy.99
  (85 shorter events, 6.1 us)
Async XLA Ops:
  8.7 10.8 %all-to-all-start = ((bf16[4,3,4,768]{3,0,1,2:T(4,128)(2,1)}), bf16[4,3,4,768]{3,0,1,2:T(4,128)(2,1)S(1)}, u32[]{:S(2)}, u32[]{:S(2)}) async-start(bf16[4,3,4,768]{3,0,1,2:T(4,128)(2,1)} %copy.73), calls=%async_computation | async-start | bytes 147456 | tf_op jit(solution)/shard_map/all_to_all | solution.py:120
  16.5 1.5 copy-start.9
  16.5 2.3 copy-start.8
  19.5 24.9 %all-to-all-start.1 = ((bf16[96,3,4,768]{3,0,1,2:T(8,128)(2,1)}), bf16[96,3,4,768]{3,0,1,2:T(8,128)(2,1)S(1)}, u32[]{:S(2)}, u32[]{:S(2)}) async-start(bf16[96,3,4,768]{3,0,1,2:T(8,128)(2,1)} %copy.75), calls=%async_computation.1 | async-start | bytes 3538944 | tf_op jit(solution)/shard_map/all_to_all | solution.py:113
  23.1 222.8 %all-gather.3.cloned.1.call-start = ((), (), s32[]{:S(2)}) async-start(), calls=%async_computation.4 | async-start | bytes 20275200 | tf_op jit(solution)/shard_map/all_gather | solution.py:143
  24.5 20.0 %copy-start.4 = (bf16[16,3,6,128]{3,2,0,1:T(8,128)(2,1)}, bf16[16,3,6,128]{3,2,0,1:T(8,128)(2,1)S(1)}, u32[]{:S(2)}) copy-start(bf16[16,3,6,128]{3,2,0,1:T(8,128)(2,1)S(1)} %reshape.244) | copy-start | bytes 221188
  55.8 2.1 copy-start
  59.4 2.1 copy-start.3
  59.4 2.2 copy-start.2
  61.7 1.9 copy-start.5
  61.7 1.9 copy-start.6
  66.7 1.6 copy-start.1
  69.8 350.8 %all-gather.5.cloned.1.call-start = ((), (), s32[]{:S(2)}) async-start(), calls=%async_computation.5 | async-start | bytes 20275200 | tf_op jit(solution)/shard_map/all_gather | solution.py:144
  70.8 1.2 copy-start.7
  635.5 7.5 %all-to-all-start.3 = ((bf16[4,2,1536]{2,1,0:T(2,128)(2,1)}), bf16[4,2,1536]{2,1,0:T(2,128)(2,1)S(1)}, u32[]{:S(2)}, u32[]{:S(2)}) async-start(bf16[4,2,1536]{2,1,0:T(2,128)(2,1)} %reshape.260), calls=%async_computation.3 | async-start | bytes 49152 | tf_op jit(solution)/shard_map/all_to_all | solution.py:174
  643.0 12.9 %all-to-all-start.2 = ((bf16[4,2,36864]{2,1,0:T(2,128)(2,1)}), bf16[4,2,36864]{2,1,0:T(2,128)(2,1)S(1)}, u32[]{:S(2)}, u32[]{:S(2)}) async-start(bf16[4,2,36864]{2,1,0:T(2,128)(2,1)} %reshape.258), calls=%async_computation.2 | async-start | bytes 1179648 | tf_op jit(solution)/shard_map/all_to_all | solution.py:167
Sparse Core Ops, SparseCore 0:
  69.9 175.9 all-gather.2
  248.9 171.6 all-gather.4
where the time goes:
time: 666 us; the launch traced here: 665 us
  waiting for transfers between devices  373 us (56%)
  matrix products  145 us (22%)
  other arithmetic  83.3 us (13%)
  local copies, waits for them, and re-layouts  31.8 us (5%)
  starting transfers between devices  17.1 us (3%)
  between operations  14.4 us (2%)
    all_gather x1, waiting for transfers between devices, local(): lax.all_gather(values_here, 'blk', axis=0, tiled=True)  175 us
    all_gather x1, waiting for transfers between devices, local(): lax.all_gather(keys_here, 'blk', axis=0, tiled=True)  171 us
    dot_general x8, matrix products, absorb(): jnp.einsum('qhd,khd->qhk', queries, key_block, preferred_element_type=jnp...  77.5 us
    dot_general x8, matrix products, absorb(): jnp.einsum('qhk,khd->qhd', weights.astype(jnp.bfloat16), value_block, pre...  67.4 us
    reduce_sum x8, other arithmetic, absorb(): new_sum = running_sum * rescale + jnp.sum(weights, axis=-1)  66.8 us
    all_to_all x1, waiting for transfers between devices, local(): lax.all_to_all(img_qkv.reshape(img_rows, 3, groups, local_width), 'head',...  18.3 us
  transfers between devices with their start and end apart: 6, of which 5 were waited for; matrix products, arithmetic and copies ran while one was open for 2% of the time, Pallas kernels for 0%

commit v1 on v0

v1 whole, which is shorter than its diff:
```python
import functools

import jax
import jax.numpy as jnp
from jax import lax
from jax.experimental import pallas as pl
from jax.experimental.pallas import tpu as pltpu
from jax.sharding import PartitionSpec as P

HEADS = 24
HD = 128
GRID_W = 128
EPSILON = 1e-06
GROUPS = 4
LH = HEADS // GROUPS
MESH = pl.DeviceIdType.MESH
LOG2E = 1.4426950408889634
BF = jnp.bfloat16
F32 = jnp.float32


def axis_freqs(pair_count):
    return 10000.0 ** (-(jnp.arange(pair_count, dtype=jnp.float32) / pair_count))


def dot(a, b, dims):
    return lax.dot_general(a, b, (dims, ((), ())), preferred_element_type=jnp.float32)


def kernel(
    img_ref, txt_ref, gain_ref, freq_ref, out_img, out_txt,
    kv_send, q_send, tx_f32, tx_send, tx_land, kv_all, q_all, s_a, s_b,
    o_send, l_send, o_land, l_land, o_own, l_own, result, txt_land,
    cs_ref, max_ref,
    loc_sem, tl_sem, zkv_s, zkv_r, zq_s, zq_r, zt_s, zt_r,
    xs_s, xs_r, xf_s, xf_r, sb_s, sb_r, yq_s, yq_r, yo_s, yo_r, yl_s, yl_r,
    hi_s, hi_r, ht_s, ht_r, hl_sem,
):
    rows = img_ref.shape[0]
    trows = txt_ref.shape[0]
    blk_rows = GROUPS * (rows + trows)
    img_part = GROUPS * rows
    width = HEADS * HD
    blk = lax.axis_index("blk")
    head = lax.axis_index("head")
    y = blk // 8
    x = ((blk // 4) % 2) * 2 + head // 2
    z = blk % 4
    c = head % 2

    def at(xx, yy, zz, cc):
        return ((yy % 4) * 8 + ((xx % 4) // 2) * 4 + zz % 4, (xx % 2) * 2 + cc)

    def al(v, n):
        return pl.multiple_of(v, n)

    partners = [at(x, y, z + d, c) for d in (1, 2, 3)]
    partners += [at(x, y + d, z, c) for d in (1, 2, 3)]
    partners += [at(x + 1, y, z, c), at(x + 3, y, z, c), at(x, y, z, 1 - c)]
    barrier = pltpu.get_barrier_semaphore()
    for p in partners:
        pl.semaphore_signal(barrier, inc=1, device_id=p, device_id_type=MESH)

    def rc(src, dst, ss, rs, to):
        return pltpu.make_async_remote_copy(
            src_ref=src, dst_ref=dst, send_sem=ss, recv_sem=rs, device_id=to, device_id_type=MESH
        )

    def kv_block(h, which):
        return kv_all.at[h, :, pl.ds(al(which * blk_rows, 16), blk_rows), :]

    def slot(xx, cc):
        return (xx % 4) * 2 + cc

    own = slot(x, c)

    def zkv(h, d, frm):
        return rc(
            kv_send.at[(z + d) % 4, h],
            kv_all.at[h, :, pl.ds(al(own * blk_rows + frm * rows, 16), rows), :],
            zkv_s.at[h, d - 1], zkv_r.at[h, d - 1], at(x, y, z + d, c),
        )

    def zq(h, d, frm):
        return rc(
            q_send.at[(z + d) % 4, h],
            q_all.at[h, y, pl.ds(al(frm * rows, 16), rows), :],
            zq_s.at[h, d - 1], zq_r.at[h, d - 1], at(x, y, z + d, c),
        )

    def zt(d, frm):
        return rc(
            tx_send.at[(z + d) % 4], tx_land.at[frm],
            zt_s.at[d - 1], zt_r.at[d - 1], at(x, y, z + d, c),
        )

    def lkv(h):
        return pltpu.make_async_copy(
            kv_send.at[z, h],
            kv_all.at[h, :, pl.ds(al(own * blk_rows + z * rows, 16), rows), :],
            loc_sem.at[h, 0],
        )

    def lq(h):
        return pltpu.make_async_copy(
            q_send.at[z, h], q_all.at[h, y, pl.ds(al(z * rows, 16), rows), :], loc_sem.at[h, 1]
        )

    def xs(h, i, which):
        b = kv_block(h, which)
        return rc(b, b, xs_s.at[h, i], xs_r.at[h, i], at(x + (1 if i == 0 else 3), y, z, c))

    def xf(h, i, which):
        b = kv_all.at[h, i, pl.ds(al(which * blk_rows, 16), blk_rows), :]
        return rc(b, b, xf_s.at[h, i], xf_r.at[h, i], at(x + (1 if i == 0 else 3), y, z, c))

    def sb(h, i, which):
        b = kv_block(h, which)
        return rc(b, b, sb_s.at[h, i], sb_r.at[h, i], at(x, y, z, 1 - c))

    def yq(h, d, frm):
        b = q_all.at[h, frm]
        return rc(b, b, yq_s.at[h, d - 1], yq_r.at[h, d - 1], at(x, y + d, z, c))

    def yo(h, i):
        return rc(
            o_send.at[h, i], o_land.at[h, i], yo_s.at[h, i], yo_r.at[h, i], at(x, y + i + 1, z, c)
        )

    def yl(h, i):
        return rc(
            l_send.at[h, i], l_land.at[h, i], yl_s.at[h, i], yl_r.at[h, i], at(x, y + i + 1, z, c)
        )

    def hi(h, d, frm):
        return rc(
            result.at[h, pl.ds(al(((z + d) % 4) * rows, 16), rows), :],
            out_img.at[:, pl.ds(al((frm * LH + h) * HD, HD), HD)],
            hi_s.at[h, d - 1], hi_r.at[h, d - 1], at(x, y, z + d, c),
        )

    def ht(h, d, frm):
        return rc(
            result.at[h, pl.ds(img_part, GROUPS * trows), :],
            txt_land.at[:, pl.ds(al((frm * LH + h) * HD, HD), HD)],
            ht_s.at[h, d - 1], ht_r.at[h, d - 1], at(x, y, z + d, c),
        )

    def hl(h, i):
        lanes = pl.ds(al((z * LH + h) * HD, HD), HD)
        if i == 0:
            return pltpu.make_async_copy(
                result.at[h, pl.ds(al(z * rows, 16), rows), :], out_img.at[:, lanes], hl_sem.at[h, 0]
            )
        return pltpu.make_async_copy(
            result.at[h, pl.ds(img_part, GROUPS * trows), :], txt_land.at[:, lanes], hl_sem.at[h, 1]
        )

    device = blk * 4 + head
    half_devices = 64
    lane = lax.broadcasted_iota(jnp.int32, (rows, HD), 1)
    pair = lane // 2
    within = (device % half_devices) * rows + lax.broadcasted_iota(jnp.int32, (rows, HD), 0)
    frame_pairs = HD // 16
    side_pairs = (HD // 2 - frame_pairs) // 2
    frame_pos = jnp.full((rows, HD), device // half_devices, jnp.int32)
    position = jnp.where(
        pair < frame_pairs,
        frame_pos,
        jnp.where(pair < frame_pairs + side_pairs, within // GRID_W, within % GRID_W),
    )
    angles = position.astype(F32) * freq_ref[0:1, :]
    cs_ref[0] = jnp.cos(angles)
    cs_ref[1] = jnp.where(lane % 2 == 0, -1.0, 1.0) * jnp.sin(angles)

    def normal(v, gain):
        return v * lax.rsqrt(jnp.mean(v * v, axis=-1, keepdims=True) + EPSILON) * gain

    def rope(v):
        even = lax.broadcasted_iota(jnp.int32, v.shape, 1) % 2 == 0
        swapped = jnp.where(even, pltpu.roll(v, HD - 1, 1), pltpu.roll(v, 1, 1))
        return cs_ref[0] * v + cs_ref[1] * swapped

    for g in range(GROUPS):
        for part in range(3):
            for h in range(LH):
                lo = part * width + (g * LH + h) * HD
                v = txt_ref[:, lo : lo + HD].astype(F32)
                if part < 2:
                    v = normal(v, gain_ref[part : part + 1, :])
                r = part * LH * trows + h * trows
                tx_f32[g, r : r + trows, :] = v
        used = 3 * LH * trows
        tx_f32[g, used:, :] = jnp.zeros((tx_f32.shape[1] - used, HD), F32)
        tx_send[g] = tx_f32[g].astype(BF)

    pl.semaphore_wait(barrier, len(partners))
    for d in (1, 2, 3):
        zt(d, z).start()
    tl = pltpu.make_async_copy(tx_send.at[z], tx_land.at[z], tl_sem)
    tl.start()

    def prep(h, carry):
        for g in range(GROUPS):
            base = (g * LH + h) * HD
            k = img_ref[:, pl.ds(al(width + base, HD), HD)].astype(F32)
            kv_send[g, h, 0] = rope(normal(k, gain_ref[1:2, :])).astype(BF)
            kv_send[g, h, 1] = img_ref[:, pl.ds(al(2 * width + base, HD), HD)]
            q = img_ref[:, pl.ds(al(base, HD), HD)].astype(F32)
            q_send[g, h] = rope(normal(q, gain_ref[0:1, :])).astype(BF)
        for d in (1, 2, 3):
            zkv(h, d, z).start()
        for d in (1, 2, 3):
            zq(h, d, z).start()
        lkv(h).start()
        lq(h).start()
        return carry

    lax.fori_loop(0, LH, prep, 0)

    for d in (1, 2, 3):
        zt(d, (z - d) % 4).wait_recv()
    tl.wait()
    pad = tx_land.shape[1]
    tr = GROUPS * trows
    row = lax.broadcasted_iota(jnp.int32, (tr, GROUPS * pad), 0)
    col = lax.broadcasted_iota(jnp.int32, (tr, GROUPS * pad), 1)
    target = (row // trows) * pad + row % trows
    pick = jnp.concatenate(
        [
            jnp.where(col == target + j * trows, 1.0, 0.0).astype(BF)
            for j in range(3 * LH)
        ],
        axis=0,
    )
    texts = dot(pick, tx_land[...].reshape(GROUPS * pad, HD), ((1,), (0,))).astype(BF)
    for h in range(LH):
        q_all[h, y, img_part:, :] = texts[h * tr : (h + 1) * tr]
        for part in (0, 1):
            r = ((part + 1) * LH + h) * tr
            kv_all[h, part, pl.ds(al(own * blk_rows + img_part, 16), tr), :] = texts[r : r + tr]

    def stage_a(h):
        for d in (1, 2, 3):
            zkv(h, d, (z - d) % 4).wait_recv()
        lkv(h).wait()
        xs(h, 0, own).start()
        xs(h, 1, own).start()
        sb(h, 0, own).start()
        for d in (1, 2, 3):
            zq(h, d, (z - d) % 4).wait_recv()
        lq(h).wait()
        for d in (1, 2, 3):
            yq(h, d, y).start()

    def stage_b(h):
        left, right = slot(x + 3, c), slot(x + 1, c)
        xs(h, 0, left).wait_recv()
        xf(h, 0, left).start()
        xs(h, 1, right).wait_recv()
        xf(h, 1, right).start()
        sb(h, 1, left).start()
        sb(h, 2, right).start()

    def stage_c(h):
        far = slot(x + 2, c)
        xf(h, 0, far).wait_recv()
        xf(h, 1, far).wait_recv()
        sb(h, 3, far).start()

    def stage_d(h):
        for i, dx in enumerate((0, 3, 1, 2)):
            sb(h, i, slot(x + dx, 1 - c)).wait_recv()
        for d in (1, 2, 3):
            yq(h, d, (y - d) % 4).wait_recv()

    scale = LOG2E * HD**-0.5
    n_keys = kv_all.shape[2]

    def fill(h, i, s_ref):
        q = q_all[h, (y + i + 1) % 4].astype(F32) * scale
        high = q.astype(BF)
        low = (q - high.astype(F32)).astype(BF)
        k = kv_all[h, 0]
        s = dot(
            jnp.concatenate([high, low], axis=1), jnp.concatenate([k, k], axis=1), ((1,), (1,))
        )
        s_ref[...] = s
        top = s[:, 0:HD]
        for t in range(1, n_keys // HD):
            top = jnp.maximum(top, s[:, t * HD : (t + 1) * HD])
        return top

    eye = lax.broadcasted_iota(jnp.int32, (HD, HD), 0) == lax.broadcasted_iota(
        jnp.int32, (HD, HD), 1
    )

    def rows_to_lanes(v):
        lines = []
        for r in range(0, blk_rows, HD):
            n = min(HD, blk_rows - r)
            lines.append(jnp.sum(jnp.where(eye[:n], v[r : r + n], 0.0), axis=0, keepdims=True))
        lines.append(jnp.zeros((8 - len(lines), HD), F32))
        return jnp.concatenate(lines, axis=0)

    def lanes_to_rows(v):
        parts = []
        for j, r in enumerate(range(0, blk_rows, HD)):
            n = min(HD, blk_rows - r)
            line = jnp.broadcast_to(v[j : j + 1], (n, HD))
            parts.append(jnp.sum(jnp.where(eye[:n], line, 0.0), axis=1, keepdims=True))
        return jnp.concatenate(parts, axis=0)

    def step(h, i, s_in, s_out, h_next, i_next):
        m = jnp.max(max_ref[...], axis=1, keepdims=True)
        top = fill(h_next, i_next, s_out)
        p = jnp.exp2(s_in[...] - m).astype(BF)
        v = kv_all[h, 1]
        acc = dot(p, jnp.concatenate([v, jnp.ones_like(v)], axis=1), ((1,), (0,)))
        max_ref[...] = top
        total = acc[:, HD:]
        o = (acc[:, :HD] / total).astype(BF)
        lse = m + jnp.log2(total)
        if i < 3:
            o_send[h, i] = o
            l_send[h, i] = rows_to_lanes(lse)
            yo(h, i).start()
            yl(h, i).start()
        else:
            o_own[...] = o
            l_own[...] = lse

    def combine(h):
        for i in range(3):
            yo(h, i).wait_recv()
            yl(h, i).wait_recv()
        ls = [l_own[...]] + [lanes_to_rows(l_land[h, i]) for i in range(3)]
        top = functools.reduce(jnp.maximum, ls)
        ws = [jnp.exp2(v - top) for v in ls]
        norm = 1.0 / (ws[0] + ws[1] + ws[2] + ws[3])
        o = o_own[...].astype(F32) * ws[0]
        for i in range(3):
            o = o + o_land[h, i].astype(F32) * ws[i + 1]
        result[h] = (o * norm).astype(BF)
        for d in (1, 2, 3):
            hi(h, d, z).start()
            ht(h, d, z).start()
        hl(h, 0).start()
        hl(h, 1).start()

    stage_a(0)
    stage_a(1)
    stage_b(0)
    stage_c(0)
    stage_a(2)
    stage_d(0)
    max_ref[...] = fill(0, 0, s_a)

    def one_head(h, carry):
        last = LH - 1

        @pl.when(h < last)
        def _():
            stage_b(h + 1)

        step(h, 0, s_a, s_b, h, 1)

        @pl.when(h + 3 <= last)
        def _():
            stage_a(h + 3)

        @pl.when(h > 0)
        def _():
            combine(h - 1)

        step(h, 1, s_b, s_a, h, 2)

        @pl.when(h < last)
        def _():
            stage_c(h + 1)

        step(h, 2, s_a, s_b, h, 3)

        @pl.when(h < last)
        def _():
            stage_d(h + 1)

        step(h, 3, s_b, s_a, jnp.minimum(h + 1, last), 0)
        return carry

    lax.fori_loop(0, LH, one_head, 0)
    combine(LH - 1)

    def arrive(h, carry):
        for d in (1, 2, 3):
            hi(h, d, (z - d) % 4).wait_recv()
            ht(h, d, (z - d) % 4).wait_recv()
        hl(h, 0).wait()
        hl(h, 1).wait()
        return carry

    lax.fori_loop(0, LH, arrive, 0)
    r8 = lax.broadcasted_iota(jnp.int32, (8, tr), 0)
    c8 = lax.broadcasted_iota(jnp.int32, (8, tr), 1)
    mine = jnp.where(c8 == r8 + z * trows, 1.0, 0.0).astype(BF)
    out_txt[...] = dot(mine, txt_land[...], ((1,), (0,)))[:trows].astype(BF)

    def sent(h, carry):
        for d in (1, 2, 3):
            zkv(h, d, z).wait_send()
            zq(h, d, z).wait_send()
            yq(h, d, y).wait_send()
            hi(h, d, z).wait_send()
            ht(h, d, z).wait_send()
            yo(h, d - 1).wait_send()
            yl(h, d - 1).wait_send()
        for i in (0, 1):
            xs(h, i, own).wait_send()
            xf(h, i, own).wait_send()
        for i in range(4):
            sb(h, i, own).wait_send()
        return carry

    lax.fori_loop(0, LH, sent, 0)
    for d in (1, 2, 3):
        zt(d, z).wait_send()


def local(img_qkv, txt_qkv, q_gain, k_gain):
    rows, trows = img_qkv.shape[0], txt_qkv.shape[0]
    width = HEADS * HD
    blk_rows = GROUPS * (rows + trows)
    n_keys = 8 * blk_rows
    pad = -(-3 * LH * trows // 16) * 16
    gains = jnp.concatenate([q_gain[None], k_gain[None], jnp.zeros((6, HD), F32)], axis=0)
    frame_pairs = HD // 16
    side_pairs = (HD // 2 - frame_pairs) // 2
    freqs = jnp.concatenate(
        [axis_freqs(frame_pairs), axis_freqs(side_pairs), axis_freqs(side_pairs)]
    )
    freqs = jnp.broadcast_to(jnp.repeat(freqs, 2)[None, :], (8, HD))
    dma = pltpu.SemaphoreType.DMA
    vm = pltpu.VMEM
    return pl.pallas_call(
        kernel,
        out_shape=(
            jax.ShapeDtypeStruct((rows, width), BF),
            jax.ShapeDtypeStruct((trows, width), BF),
        ),
        in_specs=[pl.BlockSpec(memory_space=pltpu.VMEM)] * 4,
        out_specs=(pl.BlockSpec(memory_space=pltpu.VMEM),) * 2,
        scratch_shapes=[
            vm((GROUPS, LH, 2, rows, HD), BF),
            vm((GROUPS, LH, rows, HD), BF),
            vm((GROUPS, pad, HD), F32),
            vm((GROUPS, pad, HD), BF),
            vm((GROUPS, pad, HD), BF),
            vm((LH, 2, n_keys, HD), BF),
            vm((LH, 4, blk_rows, HD), BF),
            vm((blk_rows, n_keys), F32),
            vm((blk_rows, n_keys), F32),
            vm((LH, 3, blk_rows, HD), BF),
            vm((LH, 3, 8, HD), F32),
            vm((LH, 3, blk_rows, HD), BF),
            vm((LH, 3, 8, HD), F32),
            vm((blk_rows, HD), BF),
            vm((blk_rows, HD), F32),
            vm((LH, blk_rows, HD), BF),
            vm((GROUPS * trows, width), BF),
            vm((2, rows, HD), F32),
            vm((blk_rows, HD), F32),
            dma((LH, 2)), dma,
            dma((LH, 3)), dma((LH, 3)), dma((LH, 3)), dma((LH, 3)), dma((3,)), dma((3,)),
            dma((LH, 2)), dma((LH, 2)), dma((LH, 2)), dma((LH, 2)),
            dma((LH, 4)), dma((LH, 4)),
            dma((LH, 3)), dma((LH, 3)), dma((LH, 3)), dma((LH, 3)), dma((LH, 3)), dma((LH, 3)),
            dma((LH, 3)), dma((LH, 3)), dma((LH, 3)), dma((LH, 3)), dma((LH, 2)),
        ],
        compiler_params=pltpu.CompilerParams(
            collective_id=0, has_side_effects=True, vmem_limit_bytes=56 * 2**20
        ),
        cost_estimate=pl.CostEstimate(
            flops=4 * LH * 4 * blk_rows * n_keys * HD,
            bytes_accessed=4 * rows * 3 * width,
            transcendentals=LH * 4 * blk_rows * n_keys,
        ),
    )(img_qkv, txt_qkv, gains, freqs)


def solution(mesh):
    in_specs = (P(("blk", "head"), None), P(("blk", "head"), None), P(), P())
    out_specs = (P(("blk", "head"), None), P(("blk", "head"), None))
    return jax.shard_map(local, mesh=mesh, in_specs=in_specs, out_specs=out_specs, check_vma=False)
```

time: 666 us -> 103 us (0.15)
  waiting for transfers between devices: 373 us -> 0 us
  matrix products: 145 us -> 0 us
  Pallas kernels: 0 us -> 96.2 us
  other arithmetic: 83.3 us -> 1.44 us
  local copies, waits for them, and re-layouts: 31.8 us -> 4.16 us
  starting transfers between devices: 17.1 us -> 0 us
  between operations: 14.4 us -> 0.65 us
    all_gather x2 -> x0, waiting for transfers between devices: 346 us -> none  [the longest x1 175 us: local(): lax.all_gather(values_here, 'blk', axis=0, tiled=True)]
    dot_general x16 -> x0, matrix products: 145 us -> none  [the longest x8 77.5 us: absorb(): jnp.einsum('qhd,khd->qhk', queries, key_block, preferred_element_type=jnp...]
    pallas_call x0 -> x1, Pallas kernels: none -> 96.2 us  [local(): pl.pallas_call(kernel, out_shape=(jax.ShapeDtypeStruct((rows, width), BF)...]
    reduce_sum x10 -> x0, other arithmetic: 68.4 us -> none  [the longest x8 66.8 us: absorb(): new_sum = running_sum * rescale + jnp.sum(weights, axis=-1)]
    all_to_all x4 -> x0, waiting for transfers between devices: 26.8 us -> none  [the longest x1 18.3 us: local(): lax.all_to_all(img_qkv.reshape(img_rows, 3, groups, local_width), 'head',...]
    all_to_all x4 -> x0, starting transfers between devices: 16.8 us -> none  [the longest x1 4.68 us: local(): lax.all_to_all(txt_qkv.reshape(txt_rows, 3, groups, local_width), 'head',...]
    reshape x7 -> x0, local copies, waits for them, and re-layouts: 10.2 us -> none  [the longest x2 4.5 us: local(): img_qkv.reshape(img_rows, 3, groups, local_width)]
    convert_element_type x8 -> x0, local copies, waits for them, and re-layouts: 9.89 us -> none  [the longest x4 8.44 us: normalize(): projected = projected.astype(jnp.float32)]
  transfers between devices with their start and end apart: 6 -> 0, of which waited for: 5 -> 0; matrix products, arithmetic and copies ran while one was open for 2% -> 0% of each run, Pallas kernels for 0% -> 0%
where the time goes in v1:
time: 103 us; the launch traced here: 102 us
  Pallas kernels  96.2 us (93%)
  local copies, waits for them, and re-layouts  4.16 us (4%)
  other arithmetic  1.44 us (1%)
    pallas_call x1, Pallas kernels, local(): pl.pallas_call(kernel, out_shape=(jax.ShapeDtypeStruct((rows, width), BF)...  96.2 us
    unnamed x2, local copies, waits for them, and re-layouts  3.27 us

profile of v1, /device:TPU:1, one launch (start us, length us, event | category | flops | bytes accessed | tf_op | source)
XLA Modules:
  0.0 102.5 jit_solution(18076331472194755373)
XLA Ops:
  0.6 0.1 pad.5.clone
  0.7 0.1 pad_maximum_fusion
  0.8 1.3 %maximum_maximum_fusion.gain_ref = f32[8,128]{1,0:T(8,128)} fusion(f32[1,128]{1,0:T(1,128)} %bitcast.2, f32[1,128]{1,0:T(1,128)} %bitcast.3, f32[8]{0:T(128)S(1)} %pad.5.clone), kind=kLoop, calls=%fused_computation | loop fusion | flops 2048 | bytes 5152 | tf_op jit(solution)/shard_map/concatenate | solution.py:435
  2.2 0.1 broadcast_in_dim.22
  2.2 0.1 broadcast_in_dim.23
  2.4 0.6 broadcast_in_dim.24.freq_ref
  3.0 96.2 %shard_map.59 = (bf16[96,3072]{1,0:T(8,128)(2,1)}, bf16[4,3072]{1,0:T(4,128)(2,1)}) custom-call(bf16[96,9216]{1,0:T(8,128)(2,1)} %img_ref.1, bf16[4,9216]{1,0:T(4,128)(2,1)} %txt_ref.1, f32[8,128]{1,0:T(8,128)} %maximum_maximum_fusion.gain_ref, f32[8,128]{1,0:T(8,128)} %broadcast_in_dim.24.freq_ref), custom_call_target="tpu_custom_call" | custom-call | flops 15728640000 | bytes 3538944 | tf_op jit(solution)/shard_map/pallas_call | solution.py:444
  99.2 1.9 %copy.8 = bf16[96,3072]{1,0:T(8,128)(2,1)} copy(bf16[96,3072]{1,0:T(8,128)(2,1)} %get-tuple-element.4) | data formatting | bytes 1179648
  101.1 1.4 %copy.9 = bf16[4,3072]{1,0:T(4,128)(2,1)} copy(bf16[4,3072]{1,0:T(4,128)(2,1)} %get-tuple-element.5) | data formatting | bytes 49152
  (3 shorter events, 0.0 us)
